TPU v7x, 256 devices: a whole 4x4x8 slice. The times are simulated.
256 devices in a mesh: half: 2 (over core), member: 16 (over y, x), tile: 8 (over z).
Axes of the slice: x: 4, y: 4, z: 8, core: 2. Of those that a mesh axis runs over, the one named last changes fastest.
Arguments:
- state: float32 [32, 16, 512, 1024], P(('half', 'member'), None, 'tile'), may hold values from -6 to 6
- weights: float32 [32, 512, 1024], P(('half', 'member'), 'tile'), may hold values from -6 to 6
- land_mask: int32 [512, 1024], P('tile'), may hold values 0 or 1
- level_gain: float32 [16], replicated, may hold values from 0.3 to 1
- depth: float32 [16], replicated, may hold values from 0.5 to 2
- obs_row: int32 [131072], P('tile'), may hold values from 1 to 62
- obs_col: int32 [131072], P('tile'), may hold values from 0 to 1023
- obs_quad: int32 [131072], P('tile'), may hold values from 0 to 3
- obs_frac: float32 [2, 131072], P(None, 'tile'), may hold values from 0 to 1
- obs_value: float32 [131072], P('tile'), may hold values from -6 to 6
- obs_error: float32 [131072], P('tile'), may hold values from 0.3 to 3
- noise: float32 [32, 131072], P(('half', 'member'), 'tile'), may hold values from -6 to 6
Outputs:
- stepped: float32 [32, 16, 512, 1024], P(('half', 'member'), None, 'tile')
- new_weights: float32 [32, 512, 1024], P(('half', 'member'), 'tile')
- misfit: float32 [32, 131072], P(None, ('half', 'member', 'tile'))
All inputs are finite; a program needn't handle non-finite values. No bound on the sum of `land_mask` on one device may be relied on, other than what follows from the above.
Results may differ from a plain program's by a relative error of at most 0.000071.
Values sent between devices are 32-bit elements; how exact they have to be, the bound alone decides.
No kernel may reach another device: no remote copies, remote signals or barrier semaphores. Data moves between devices by JAX's collectives and lax.ppermute only.
A program may use at most 128 MiB of HBM per device.

v0:
```python
import math
import jax
import jax.numpy as jnp
from jax import lax
from jax.sharding import PartitionSpec as P


def with_halo(block, sides, width):
    for axis, dim in sides:
        count = lax.axis_size(axis)
        forward = [(i, i + 1) for i in range(count - 1)]
        backward = [(target, source) for source, target in forward]
        low = lax.ppermute(
            lax.slice_in_dim(block, block.shape[dim] - width, None, axis=dim), axis, forward
        )
        high = lax.ppermute(lax.slice_in_dim(block, 0, width, axis=dim), axis, backward)
        block = jnp.concatenate([low, block, high], axis=dim)
    return block


def interpolate(column, row_index, col_index, obs_quad, obs_frac):
    width = column.shape[1]
    row_step = jnp.where(obs_quad % 2 == 1, 1, -1).astype(jnp.int32)
    col_step = jnp.where(obs_quad // 2 == 1, 1, -1).astype(jnp.int32)
    row_other = row_index + row_step
    col_other = (col_index + col_step) % width
    flat = column.reshape(-1)
    corner_aa = jnp.take(flat, row_index * width + col_index)
    corner_ab = jnp.take(flat, row_index * width + col_other)
    corner_ba = jnp.take(flat, row_other * width + col_index)
    corner_bb = jnp.take(flat, row_other * width + col_other)
    first = obs_frac[0]
    second = obs_frac[1]
    return (
        (1.0 - first) * (1.0 - second) * corner_aa
        + (1.0 - first) * second * corner_ab
        + first * (1.0 - second) * corner_ba
        + first * second * corner_bb
    )


def on_device(
    state,
    weights,
    land_mask,
    level_gain,
    depth,
    obs_row,
    obs_col,
    obs_quad,
    obs_frac,
    obs_value,
    obs_error,
    noise,
):
    highest = lax.Precision.HIGHEST
    members = lax.axis_size(("half", "member"))
    member_index = lax.axis_index(("half", "member"))
    tile_count = lax.axis_size("tile")
    obs_local = obs_row.shape[0]
    shard_size = obs_local // members
    total_obs = obs_local * tile_count
    padded = with_halo(state, (("tile", 2),), 1)
    laplacian = (
        padded[:, :, :-2]
        + padded[:, :, 2:]
        + jnp.roll(state, 1, axis=3)
        + jnp.roll(state, -1, axis=3)
        - 4.0 * state
    )
    diffusivity = 0.24 * jax.nn.sigmoid(weights)
    ocean_cells = land_mask.astype(jnp.float32)
    stepped = (
        state
        + level_gain[None, :, None, None] * (ocean_cells[None] * diffusivity)[:, None] * laplacian
    )
    levels_here = state.shape[1]
    column = jnp.sum(depth[:, None, None] * stepped[0], axis=0) / math.sqrt(levels_here)
    predicted = interpolate(column, obs_row, obs_col, obs_quad, obs_frac)
    perturbed = obs_value + noise[0]
    grouped, noisy_grouped = (
        lax.all_to_all(
            predicted.reshape(members, shard_size),
            ("half", "member"),
            split_axis=0,
            concat_axis=0,
            tiled=True,
        ),
        lax.all_to_all(
            perturbed.reshape(members, shard_size),
            ("half", "member"),
            split_axis=0,
            concat_axis=0,
            tiled=True,
        ),
    )
    error_shard = lax.dynamic_slice_in_dim(obs_error, member_index * shard_size, shard_size, 0)
    misfit = noisy_grouped - grouped
    anomaly = grouped - jnp.mean(grouped, axis=0, keepdims=True)
    weighted = anomaly / error_shard[None]
    gram = jnp.einsum("ko,jo->kj", weighted, anomaly, precision=highest)
    products = jnp.einsum("ko,jo->kj", weighted, misfit, precision=highest)
    gram, products = lax.psum((gram, products), ("half", "member", "tile"))
    identity = jnp.eye(members, dtype=jnp.float32)
    factor = jnp.linalg.cholesky(identity + gram / total_obs)
    coefficients = jax.scipy.linalg.cho_solve((factor, True), products / total_obs)
    combination = identity + coefficients - jnp.mean(coefficients, axis=0, keepdims=True)
    own_column = lax.dynamic_slice_in_dim(combination, member_index, 1, 1)[:, 0]
    initial = jnp.zeros(weights.shape[1:], jnp.float32)
    new_weights = (
        initial
        + jnp.einsum(
            "k,krc->rc",
            own_column,
            lax.all_gather(weights, ("half", "member"), axis=0, tiled=True),
            precision=highest,
        )
    )[None]
    return (stepped, new_weights, misfit)


def solution(mesh):
    in_specs = (
        P(("half", "member"), None, "tile", None),
        P(("half", "member"), "tile", None),
        P("tile", None),
        P(),
        P(),
        P("tile"),
        P("tile"),
        P("tile"),
        P(None, "tile"),
        P("tile"),
        P("tile"),
        P(("half", "member"), "tile"),
    )
    out_specs = (
        P(("half", "member"), None, "tile", None),
        P(("half", "member"), "tile", None),
        P(None, ("half", "member", "tile")),
    )
    return jax.shard_map(
        on_device, mesh=mesh, in_specs=in_specs, out_specs=out_specs, check_vma=False
    )
```

profile of v0, /device:TPU:1, one launch (start us, length us, event | category | flops | bytes accessed | tf_op | source)
XLA Modules:
  0.0 536.1 jit_solution(11448985625103804217)
XLA Ops:
  7.2 0.0 all-gather.2.cloned.1.call-start
  7.2 0.7 all-gather.2.cloned.1.call-update
  7.9 1.3 fusion.40
  9.2 4.4 collective-permute-start
  13.6 1.3 collective-permute-start.1
  14.9 1.4 fusion.41
  16.3 1.1 broadcast_clamp_fusion.2
  17.4 0.0 copy-start.6
  17.4 0.0 copy-start
  17.4 0.0 copy-start.1
  17.4 0.0 copy-start.7
  17.4 0.0 copy-start.8
  17.4 0.0 copy-start.9
  17.5 0.0 copy-start.10
  17.5 8.0 %fusion.42 = (f32[1,16,64,1023]{3,2,1,0:T(8,128)}, f32[1,16,64,1023]{3,2,1,0:T(8,128)}) fusion(f32[1,16,64,1024]{3,2,1,0:T(8,128)} %param.14), kind=kLoop, calls=%fused_computation.86 | loop fusion | bytes 16760832 | tf_op jit(solution)/shard_map/jit(_roll_static)/slice | solution.py:67
  25.5 0.0 copy-done.6
  25.5 0.1 fusion.43
  25.6 0.0 copy-done
  25.6 0.0 copy-done.1
  25.6 0.1 fusion.9
  25.7 0.8 dynamic_slice.6
  26.5 0.0 copy-done.7
  26.5 0.0 copy-done.8
  26.5 0.6 add.116
  27.1 0.0 collective-permute-done
  27.1 0.0 collective-permute-done.1
  27.1 0.0 copy-done.9
  27.1 0.0 copy-done.10
  27.1 11.0 %fusion.8 = (f32[64,1024]{1,0:T(8,128)S(1)}, f32[1,16,64,1024]{3,2,1,0:T(8,128)}) fusion(f32[16]{0:T(128)S(1)} %copy-done.9, f32[1,16,64,1024]{3,2,1,0:T(8,128)} %param.14, f32[1,16,64,1]{3,2,1,0:T(8,128)S(1)} %get-tuple-element.13, f32[1,16,64,1023]{3,2,1,0:T(8,128)} %get-tuple-element.15, f32[1,16,64,1023]{3,2,1,0:T(8,128)} %get-tuple-element.14, ...), kind=kLoop, calls=%fused_computation.15 | loop fusion | flops 14614528 | bytes 17432704 | tf_op jit(solution)/shard_map/reduce_sum | solution.py:78
  38.2 90.5 %gather_fusion = f32[16384]{0:T(1024)S(1)} fusion(f32[65536]{0:T(1024)S(1)} %bitcast.48, s32[16384]{0:T(1024)S(1)} %get-tuple-element.21), kind=kCustom, calls=%fused_computation.clone | custom fusion | bytes 196608 | tf_op jit(solution)/shard_map/jit(_take)/gather | solution.py:28
  128.8 90.5 %gather_fusion.1 = f32[16384]{0:T(1024)S(1)} fusion(f32[65536]{0:T(1024)S(1)} %bitcast.49, s32[16384]{0:T(1024)S(1)} %get-tuple-element.16), kind=kCustom, calls=%fused_computation.1.clone | custom fusion | bytes 196608 | tf_op jit(solution)/shard_map/jit(_take)/gather | solution.py:29
  219.3 90.5 %gather_fusion.2 = f32[16384]{0:T(1024)S(1)} fusion(f32[65536]{0:T(1024)S(1)} %bitcast.50, s32[16384]{0:T(1024)S(1)} %get-tuple-element.18), kind=kCustom, calls=%fused_computation.2.clone | custom fusion | bytes 196608 | tf_op jit(solution)/shard_map/jit(_take)/gather | solution.py:30
  309.8 0.0 copy-start.2
  309.9 0.0 copy-start.3
  309.9 0.0 copy-start.4
  309.9 90.5 %gather_fusion.3 = f32[16384]{0:T(1024)S(1)} fusion(f32[65536]{0:T(1024)S(1)} %bitcast.51, s32[16384]{0:T(1024)S(1)} %get-tuple-element.17), kind=kCustom, calls=%fused_computation.3.clone | custom fusion | bytes 196608 | tf_op jit(solution)/shard_map/jit(_take)/gather | solution.py:31
  400.4 0.0 copy-done.2
  400.4 0.0 copy-done.3
  400.4 0.0 copy-done.4
  400.5 0.8 fusion.19
  401.3 8.1 %all-to-all-start = ((f32[32,1,512]{2,1,0:T(1,128)}), f32[32,1,512]{2,1,0:T(1,128)S(1)}, u32[]{:S(2)}, u32[]{:S(2)}) async-start(f32[32,1,512]{2,1,0:T(1,128)} %bitcast.5), calls=%async_computation | async-start | bytes 131072 | tf_op jit(solution)/shard_map/all_to_all | solution.py:82
  409.4 7.1 %all-to-all-done = f32[32,1,512]{2,1,0:T(1,128)S(1)} async-done(((f32[32,1,512]{2,1,0:T(1,128)}), f32[32,1,512]{2,1,0:T(1,128)S(1)}, u32[]{:S(2)}, u32[]{:S(2)}) %all-to-all-start) | async-done | bytes 65568 | tf_op jit(solution)/shard_map/all_to_all | solution.py:82
  416.5 4.2 all-to-all-start.1
  420.7 0.1 reduce_sum.28
  420.8 7.0 %all-to-all-done.1 = f32[32,1,512]{2,1,0:T(1,128)S(1)} async-done(((f32[32,1,512]{2,1,0:T(1,128)}), f32[32,1,512]{2,1,0:T(1,128)S(1)}, u32[]{:S(2)}, u32[]{:S(2)}) %all-to-all-start.1) | async-done | bytes 65568 | tf_op jit(solution)/shard_map/all_to_all | solution.py:89
  427.8 0.1 broadcast_divide_fusion
  427.9 0.0 copy-start.5
  427.9 0.2 fusion.16
  428.1 0.2 fusion.13
  428.3 79.0 %all-reduce = (f32[32,32]{1,0:T(8,128)S(1)}, f32[32,32]{1,0:T(8,128)S(1)}) all-reduce(f32[32,32]{1,0:T(8,128)S(1)} %fusion.13, f32[32,32]{1,0:T(8,128)S(1)} %fusion.16), channel_id=1, replica_groups=mesh['half'=2,'member'=16,'tile'=8] {'half','member','tile'}, use_global_device_ids=true, to_apply=%region_2.4 | all-reduce | flops 2048 | bytes 16384 | tf_op jit(solution)/shard_map/psum | solution.py:103
  507.3 0.1 copy.19
  507.4 2.9 cholesky.14
  510.3 0.6 compare_reduce_fusion
  511.0 0.7 fusion.26
  511.6 2.4 custom-call.10
  514.1 0.2 fusion.31
  514.3 0.3 fusion.44
  514.6 0.1 copy.26
  514.7 0.6 dynamic-slice
  515.3 0.8 fusion.28
  516.1 0.0 all-gather.2.cloned.1.call-done
  516.2 12.3 %fusion = f32[1,64,1024]{2,0,1:T(1,128)S(1)} fusion(f32[32,64,1024]{2,1,0:T(8,128)} %all-gather.2.cloned.1.call-done, f32[32]{0:T(128)S(1)} %fusion.28), kind=kOutput, calls=%fused_computation.4 | convolution fusion | flops 25165824 | bytes 8650880 | tf_op jit(solution)/shard_map/k,krc->rc/dot_general | solution.py:112
  528.5 0.0 copy-done.5
  528.5 0.8 copy.22
  (10 shorter events, 0.2 us)
Async XLA Ops:
  7.2 509.0 %all-gather.2.cloned.1.call-start = ((), (), s32[]{:S(2)}) async-start(), calls=%async_computation.2 | async-start | bytes 8650752 | tf_op jit(solution)/shard_map/all_gather | solution.py:115
  9.2 17.9 %collective-permute-start = (f32[1,16,1,1024]{3,2,1,0:T(1,128)S(1)}, f32[1,16,1,1024]{3,2,1,0:T(1,128)S(1)}, u32[]{:S(2)}, u32[]{:S(2)}) collective-permute-start(f32[1,16,1,1024]{3,2,1,0:T(1,128)S(1)} %get-tuple-element.10), channel_id=1, source_target_pairs={{0,1},{1,2},{2,3},{3,4},{4,5},{5,6},{6,7},{8,9},{9,10},{10,11},{11... | collective-permute-start | bytes 196616 | tf_op jit(solution)/shard_map/ppermute | solution.py:13
  13.6 13.6 %collective-permute-start.1 = (f32[1,16,1,1024]{3,2,1,0:T(1,128)S(1)}, f32[1,16,1,1024]{3,2,1,0:T(1,128)S(1)}, u32[]{:S(2)}, u32[]{:S(2)}) collective-permute-start(f32[1,16,1,1024]{3,2,1,0:T(1,128)S(1)} %get-tuple-element.11), channel_id=1, source_target_pairs={{1,0},{2,1},{3,2},{4,3},{5,4},{6,5},{7,6},{9,8},{10,9},{11,10},{12... | collective-permute-start | bytes 196616 | tf_op jit(solution)/shard_map/ppermute | solution.py:16
  17.4 8.1 %copy-start.6 = (f32[2,16384]{1,0:T(2,128)S(1)}, f32[2,16384]{1,0:T(2,128)}, u32[]{:S(2)}) copy-start(f32[2,16384]{1,0:T(2,128)} %param.22) | copy-start | bytes 393220
  17.4 8.2 %copy-start = (f32[1,64,1024]{2,1,0:T(8,128)S(1)}, f32[1,64,1024]{2,1,0:T(8,128)}, u32[]{:S(2)}) copy-start(f32[1,64,1024]{2,1,0:T(8,128)} %param.15) | copy-start | bytes 786436
  17.4 8.2 %copy-start.1 = (s32[64,1024]{1,0:T(8,128)S(1)}, s32[64,1024]{1,0:T(8,128)}, u32[]{:S(2)}) copy-start(s32[64,1024]{1,0:T(8,128)} %param.16) | copy-start | bytes 786436
  17.4 9.1 %copy-start.7 = (f32[16384]{0:T(1024)S(1)}, f32[16384]{0:T(1024)}, u32[]{:S(2)}) copy-start(f32[16384]{0:T(1024)} %param.23) | copy-start | bytes 196612
  17.4 9.1 %copy-start.8 = (f32[1,16384]{1,0:T(1,128)S(1)}, f32[1,16384]{1,0:T(1,128)}, u32[]{:S(2)}) copy-start(f32[1,16384]{1,0:T(1,128)} %param.25) | copy-start | bytes 196612
  17.4 9.7 %copy-start.9 = (f32[16]{0:T(128)S(1)}, f32[16]{0:T(128)}, u32[]{:S(2)}) copy-start(f32[16]{0:T(128)} %param.18) | copy-start | bytes 196
  17.5 9.7 %copy-start.10 = (f32[16]{0:T(128)S(1)}, f32[16]{0:T(128)}, u32[]{:S(2)}) copy-start(f32[16]{0:T(128)} %param.17) | copy-start | bytes 196
  309.8 90.6 %copy-start.2 = (s32[16384]{0:T(1024)S(1)}, s32[16384]{0:T(1024)}, u32[]{:S(2)}) copy-start(s32[16384]{0:T(1024)} %param.19) | copy-start | bytes 196612
  309.9 90.6 %copy-start.3 = (s32[16384]{0:T(1024)S(1)}, s32[16384]{0:T(1024)}, u32[]{:S(2)}) copy-start(s32[16384]{0:T(1024)} %param.20) | copy-start | bytes 196612
  309.9 90.6 %copy-start.4 = (s32[16384]{0:T(1024)S(1)}, s32[16384]{0:T(1024)}, u32[]{:S(2)}) copy-start(s32[16384]{0:T(1024)} %param.21) | copy-start | bytes 196612
  401.3 15.2 %all-to-all-start = ((f32[32,1,512]{2,1,0:T(1,128)}), f32[32,1,512]{2,1,0:T(1,128)S(1)}, u32[]{:S(2)}, u32[]{:S(2)}) async-start(f32[32,1,512]{2,1,0:T(1,128)} %bitcast.5), calls=%async_computation | async-start | bytes 131072 | tf_op jit(solution)/shard_map/all_to_all | solution.py:82
  416.5 11.3 %all-to-all-start.1 = ((f32[32,1,512]{2,1,0:T(1,128)}), f32[32,1,512]{2,1,0:T(1,128)S(1)}, u32[]{:S(2)}, u32[]{:S(2)}) async-start(f32[32,1,512]{2,1,0:T(1,128)} %bitcast.10), calls=%async_computation.1 | async-start | bytes 131072 | tf_op jit(solution)/shard_map/all_to_all | solution.py:89
  427.9 100.6 %copy-start.5 = (f32[32,1,512]{2,0,1:T(8,128)}, f32[32,1,512]{2,0,1:T(8,128)S(1)}, u32[]{:S(2)}) copy-start(f32[32,1,512]{2,0,1:T(8,128)S(1)} %copy.43) | copy-start | bytes 196612
Sparse Core Ops, SparseCore 0:
  10.6 62.1 all-gather.1
where the time goes:
time: 537 us; the launch traced here: 536 us
  local copies, waits for them, and re-layouts  375 us (70%)
  blocking collectives  79 us (15%)
  other arithmetic  21.4 us (4%)
  starting transfers between devices  18 us (3%)
  waiting for transfers between devices  14.8 us (3%)
  between operations  14.4 us (3%)
  matrix products  13.2 us (2%)
    gather x1, local copies, waits for them, and re-layouts, interpolate(): corner_aa = jnp.take(flat, row_index * width + col_index)  90.5 us
    gather x1, local copies, waits for them, and re-layouts, interpolate(): corner_ab = jnp.take(flat, row_index * width + col_other)  90.5 us
    gather x1, local copies, waits for them, and re-layouts, interpolate(): corner_ba = jnp.take(flat, row_other * width + col_index)  90.5 us
    gather x1, local copies, waits for them, and re-layouts, interpolate(): corner_bb = jnp.take(flat, row_other * width + col_other)  90.5 us
    psum x1, blocking collectives, on_device(): gram, products = lax.psum((gram, products), ('half', 'member', 'tile'))  79 us
    dot_general x1, matrix products, on_device(): jnp.einsum('k,krc->rc', own_column, lax.all_gather(weights, ('half', 'mem...  12.3 us
    reduce_sum x1, other arithmetic, on_device(): jnp.sum(depth[:, None, None] * stepped[0], axis=0) / math.sqrt(levels_here)  11 us
  transfers between devices with their start and end apart: 5, of which 2 were waited for; matrix products, arithmetic and copies ran while one was open for 74% of the time, Pallas kernels for 0%

commit v1 on v0

--- a/solution.py
+++ b/solution.py
@@ -100,7 +100,7 @@
     weighted = anomaly / error_shard[None]
     gram = jnp.einsum("ko,jo->kj", weighted, anomaly, precision=highest)
     products = jnp.einsum("ko,jo->kj", weighted, misfit, precision=highest)
-    gram, products = lax.psum((gram, products), ("half", "member", "tile"))
+    gram, products = lax.psum(lax.psum((gram, products), "half"), ("member", "tile"))
     identity = jnp.eye(members, dtype=jnp.float32)
     factor = jnp.linalg.cholesky(identity + gram / total_obs)
     coefficients = jax.scipy.linalg.cho_solve((factor, True), products / total_obs)

time: 537 us -> 1150 us (2.14)
  the two profiles are of different devices: /device:TPU:1 before, /device:TPU:0 now
where the time goes in v1:
time: 1150 us
  blocking collectives  693 us (60%)
  local copies, waits for them, and re-layouts  375 us (33%)
  other arithmetic  21.3 us (2%)
  waiting for transfers between devices  15.5 us (1%)
  starting transfers between devices  14.6 us (1%)
  between operations  14.4 us (1%)
  matrix products  13.2 us (1%)
    psum x1, blocking collectives, on_device(): lax.psum(lax.psum((gram, products), 'half'), ('member', 'tile'))  690 us
    gather x1, local copies, waits for them, and re-layouts, interpolate(): corner_aa = jnp.take(flat, row_index * width + col_index)  90.5 us
    gather x1, local copies, waits for them, and re-layouts, interpolate(): corner_ab = jnp.take(flat, row_index * width + col_other)  90.5 us
    gather x1, local copies, waits for them, and re-layouts, interpolate(): corner_ba = jnp.take(flat, row_other * width + col_index)  90.5 us
    gather x1, local copies, waits for them, and re-layouts, interpolate(): corner_bb = jnp.take(flat, row_other * width + col_other)  90.5 us
  transfers between devices with their start and end apart: 5, of which 2 were waited for; matrix products, arithmetic and copies ran while one was open for 35% of the time, Pallas kernels for 0%

profile of v1, /device:TPU:0, one launch (start us, length us, event | category | flops | bytes accessed | tf_op | source)
XLA Modules:
  0.0 1147.5 jit_solution(10116088573387664088)
XLA Ops:
  7.2 0.0 all-gather.2.cloned.1.call-start
  7.2 0.7 all-gather.2.cloned.1.call-update
  7.9 1.3 fusion.40
  9.2 2.1 collective-permute-start
  11.3 1.3 collective-permute-start.1
  12.6 1.4 fusion.41
  14.0 1.1 broadcast_clamp_fusion.2
  15.1 0.0 copy-start.6
  15.1 0.0 copy-start
  15.1 0.0 copy-start.1
  15.1 0.0 copy-start.7
  15.1 0.0 copy-start.8
  15.2 0.0 copy-start.9
  15.2 0.0 copy-start.10
  15.2 8.0 fusion.42
  23.2 0.0 copy-done.6
  23.2 0.1 fusion.43
  23.3 0.0 copy-done
  23.3 0.0 copy-done.1
  23.3 0.1 fusion.9
  23.4 0.8 dynamic_slice.6
  24.2 0.0 copy-done.7
  24.2 0.0 copy-done.8
  24.2 0.6 add.120
  24.9 0.0 collective-permute-done
  24.9 0.0 collective-permute-done.1
  24.9 0.0 copy-done.9
  24.9 0.0 copy-done.10
  24.9 11.0 fusion.8
  35.9 90.5 %gather_fusion = f32[16384]{0:T(1024)S(1)} fusion(f32[65536]{0:T(1024)S(1)} %bitcast.48, s32[16384]{0:T(1024)S(1)} %get-tuple-element.23), kind=kCustom, calls=%fused_computation.clone | custom fusion | bytes 196608 | tf_op jit(solution)/shard_map/jit(_take)/gather | solution.py:28
  126.5 90.5 %gather_fusion.1 = f32[16384]{0:T(1024)S(1)} fusion(f32[65536]{0:T(1024)S(1)} %bitcast.49, s32[16384]{0:T(1024)S(1)} %get-tuple-element.18), kind=kCustom, calls=%fused_computation.1.clone | custom fusion | bytes 196608 | tf_op jit(solution)/shard_map/jit(_take)/gather | solution.py:29
  217.0 90.5 %gather_fusion.2 = f32[16384]{0:T(1024)S(1)} fusion(f32[65536]{0:T(1024)S(1)} %bitcast.50, s32[16384]{0:T(1024)S(1)} %get-tuple-element.20), kind=kCustom, calls=%fused_computation.2.clone | custom fusion | bytes 196608 | tf_op jit(solution)/shard_map/jit(_take)/gather | solution.py:30
  307.6 0.0 copy-start.2
  307.6 0.0 copy-start.3
  307.6 0.0 copy-start.4
  307.6 90.5 %gather_fusion.3 = f32[16384]{0:T(1024)S(1)} fusion(f32[65536]{0:T(1024)S(1)} %bitcast.51, s32[16384]{0:T(1024)S(1)} %get-tuple-element.19), kind=kCustom, calls=%fused_computation.3.clone | custom fusion | bytes 196608 | tf_op jit(solution)/shard_map/jit(_take)/gather | solution.py:31
  398.1 0.0 copy-done.2
  398.1 0.0 copy-done.3
  398.2 0.0 copy-done.4
  398.2 0.8 fusion.19
  399.0 7.3 all-to-all-start
  406.4 7.5 all-to-all-done
  413.8 3.9 all-to-all-start.1
  417.7 0.1 reduce_sum.28
  417.7 7.3 all-to-all-done.1
  425.1 0.1 broadcast_divide_fusion
  425.2 0.0 copy-start.5
  425.2 0.2 fusion.16
  425.4 0.2 fusion.13
  425.6 3.4 all-reduce.1
  429.0 689.7 %all-reduce = (f32[32,32]{1,0:T(8,128)S(1)}, f32[32,32]{1,0:T(8,128)S(1)}) all-reduce(f32[32,32]{1,0:T(8,128)S(1)} %get-tuple-element.6, f32[32,32]{1,0:T(8,128)S(1)} %get-tuple-element.7), channel_id=1, replica_groups=mesh['half'=2,'member'=16,'tile'=8] {'member','tile'}, use_global_device_ids=true, to_apply=%region_3.5 | all-reduce | flops 2048 | bytes 16384 | tf_op jit(solution)/shard_map/psum | solution.py:103
  1118.7 0.1 copy.19
  1118.8 2.9 cholesky.14
  1121.8 0.6 compare_reduce_fusion
  1122.4 0.7 fusion.26
  1123.1 2.4 custom-call.10
  1125.5 0.2 fusion.31
  1125.7 0.3 fusion.44
  1126.1 0.1 copy.26
  1126.2 0.6 dynamic-slice
  1126.7 0.8 fusion.28
  1127.6 0.0 all-gather.2.cloned.1.call-done
  1127.6 12.3 %fusion = f32[1,64,1024]{2,0,1:T(1,128)S(1)} fusion(f32[32,64,1024]{2,1,0:T(8,128)} %all-gather.2.cloned.1.call-done, f32[32]{0:T(128)S(1)} %fusion.28), kind=kOutput, calls=%fused_computation.4 | convolution fusion | flops 25165824 | bytes 8650880 | tf_op jit(solution)/shard_map/k,krc->rc/dot_general | solution.py:112
  1139.9 0.8 copy.22
  (11 shorter events, 0.2 us)
Async XLA Ops:
  7.2 1120.4 %all-gather.2.cloned.1.call-start = ((), (), s32[]{:S(2)}) async-start(), calls=%async_computation.2 | async-start | bytes 8650752 | tf_op jit(solution)/shard_map/all_gather | solution.py:115
  9.2 15.7 %collective-permute-start = (f32[1,16,1,1024]{3,2,1,0:T(1,128)S(1)}, f32[1,16,1,1024]{3,2,1,0:T(1,128)S(1)}, u32[]{:S(2)}, u32[]{:S(2)}) collective-permute-start(f32[1,16,1,1024]{3,2,1,0:T(1,128)S(1)} %get-tuple-element.12), channel_id=1, source_target_pairs={{0,1},{1,2},{2,3},{3,4},{4,5},{5,6},{6,7},{8,9},{9,10},{10,11},{11... | collective-permute-start | bytes 196616 | tf_op jit(solution)/shard_map/ppermute | solution.py:13
  11.3 13.6 %collective-permute-start.1 = (f32[1,16,1,1024]{3,2,1,0:T(1,128)S(1)}, f32[1,16,1,1024]{3,2,1,0:T(1,128)S(1)}, u32[]{:S(2)}, u32[]{:S(2)}) collective-permute-start(f32[1,16,1,1024]{3,2,1,0:T(1,128)S(1)} %get-tuple-element.13), channel_id=1, source_target_pairs={{1,0},{2,1},{3,2},{4,3},{5,4},{6,5},{7,6},{9,8},{10,9},{11,10},{12... | collective-permute-start | bytes 196616 | tf_op jit(solution)/shard_map/ppermute | solution.py:16
  15.1 8.1 copy-start.6
  15.1 8.2 copy-start
  15.1 8.2 copy-start.1
  15.1 9.1 copy-start.7
  15.1 9.1 copy-start.8
  15.2 9.7 copy-start.9
  15.2 9.7 copy-start.10
  307.6 90.6 %copy-start.2 = (s32[16384]{0:T(1024)S(1)}, s32[16384]{0:T(1024)}, u32[]{:S(2)}) copy-start(s32[16384]{0:T(1024)} %param.19) | copy-start | bytes 196612
  307.6 90.6 %copy-start.3 = (s32[16384]{0:T(1024)S(1)}, s32[16384]{0:T(1024)}, u32[]{:S(2)}) copy-start(s32[16384]{0:T(1024)} %param.20) | copy-start | bytes 196612
  307.6 90.6 %copy-start.4 = (s32[16384]{0:T(1024)S(1)}, s32[16384]{0:T(1024)}, u32[]{:S(2)}) copy-start(s32[16384]{0:T(1024)} %param.21) | copy-start | bytes 196612
  399.0 14.8 %all-to-all-start = ((f32[32,1,512]{2,1,0:T(1,128)}), f32[32,1,512]{2,1,0:T(1,128)S(1)}, u32[]{:S(2)}, u32[]{:S(2)}) async-start(f32[32,1,512]{2,1,0:T(1,128)} %bitcast.5), calls=%async_computation | async-start | bytes 131072 | tf_op jit(solution)/shard_map/all_to_all | solution.py:82
  413.8 11.3 all-to-all-start.1
  425.2 714.7 %copy-start.5 = (f32[32,1,512]{2,0,1:T(8,128)}, f32[32,1,512]{2,0,1:T(8,128)S(1)}, u32[]{:S(2)}) copy-start(f32[32,1,512]{2,0,1:T(8,128)S(1)} %copy.43) | copy-start | bytes 196612
Sparse Core Ops, SparseCore 0:
  10.6 59.1 all-gather.1
